TPU v7x, 512 devices: a whole 4x8x8 slice. The times are simulated.
512 devices in a mesh: grp: 16 (over x, z_hi), body: 32 (over y, z_lo, core).
Axes of the slice: x: 4, y: 8, z: 8 (z_hi: 4, z_lo: 2; z = z_hi * 2 + z_lo), core: 2. Of those that a mesh axis runs over, the one named last changes fastest.
Arguments:
- incident: bfloat16 [512, 16, 512], P(('grp', 'body')), may hold values from -6 to 6
- exciting: float32 [512, 16, 512], P(('grp', 'body')), may hold values from -6 to 6
- t_matrices: bfloat16 [512, 2, 256, 256], P(('grp', 'body')), may hold values from -0.1875 to 0.1875
- hankel_rows: bfloat16 [225, 2, 512], replicated, may hold values from -0.046875 to 0.046875
- offsets: int32 [512, 32], P(('grp', 'body')), may hold values from 0 to 224
- lattice_slots: int32 [512], P('grp'), may hold values from 0 to 31, as said below
- up_maps: bfloat16 [512, 2, 256, 512], P(('grp', 'body')), may hold values from -0.0625 to 0.0625
- down_maps: bfloat16 [512, 2, 512, 256], P(('grp', 'body')), may hold values from -0.1875 to 0.1875
- group_maps: bfloat16 [16, 16, 2, 512, 512], P('grp', None, None, 'body'), may hold values from -0.046875 to 0.046875
Outputs:
- updated: float32 [512, 16, 512], P(('grp', 'body'))
Inputs may be any that keep to these rules, and one draw needn't show every extreme that they name: `lattice_slots`: within each group the 32 columns stand at the slots 0 to 31, one column a slot.
All inputs are finite; a program needn't handle non-finite values.
Results may differ from a plain program's by a relative error of at most 0.0034.
Values may be sent and summed in bfloat16 or wider, within the bound.
A program may use at most 64 MiB of HBM per device.

v0:
```python
import math
import jax
import jax.numpy as jnp
from jax import lax
from jax.sharding import PartitionSpec as P


def complex_apply(form, values, real_mats, imag_mats):
    half_width = values.shape[-1] // 2
    real_values = values[..., :half_width]
    imag_values = values[..., half_width:]
    real_out = jnp.einsum(
        form, real_values, real_mats, preferred_element_type=jnp.float32
    ) - jnp.einsum(form, imag_values, imag_mats, preferred_element_type=jnp.float32)
    imag_out = jnp.einsum(
        form, real_values, imag_mats, preferred_element_type=jnp.float32
    ) + jnp.einsum(form, imag_values, real_mats, preferred_element_type=jnp.float32)
    return jnp.concatenate([real_out, imag_out], axis=-1)


def toeplitz_mats(sequences):
    length = sequences.shape[-1] // 2
    repeats = (1,) * (sequences.ndim - 1) + (length,)
    tiled = jnp.tile(sequences, repeats)
    window = tiled[..., length : length + length * (2 * length - 1)]
    return window.reshape(sequences.shape[:-1] + (length, 2 * length - 1))[..., :length]


def local(
    incident,
    exciting,
    t_matrices,
    hankel_rows,
    offsets,
    lattice_slots,
    up_maps,
    down_maps,
    group_maps,
):
    body_index = lax.axis_index("body")
    group_index = lax.axis_index("grp")
    local_count = incident.shape[0]
    scattered = complex_apply("iln,inm->ilm", incident, t_matrices[:, 0], t_matrices[:, 1]).astype(
        jnp.bfloat16
    )
    own_members = body_index * local_count + jnp.arange(local_count, dtype=jnp.int32)
    zero_seq = jnp.zeros((), jnp.bfloat16)
    all_offsets = lax.all_gather(offsets, "body", axis=0, tiled=True)
    group_count = lattice_slots.shape[0]
    own_slots = lax.dynamic_slice_in_dim(lattice_slots, body_index * local_count, local_count, 0)
    table_rows = jnp.take(all_offsets, own_slots, axis=1)
    sequences = jnp.take(hankel_rows, table_rows, axis=0)
    targets = jnp.arange(group_count, dtype=jnp.int32)
    keep = targets[:, None] != own_members[None, :]
    sequences = jnp.where(keep[:, :, None, None], sequences, zero_seq)
    block_rows = math.gcd(group_count, 4)
    sequences = sequences.reshape((group_count // block_rows, block_rows) + sequences.shape[1:])

    def one_block(block_seqs):
        mats = toeplitz_mats(block_seqs)
        return complex_apply("sln,tsnm->tlm", scattered, mats[:, :, 0], mats[:, :, 1])

    terms = lax.map(one_block, sequences)
    totals = lax.psum(terms.reshape((group_count,) + terms.shape[2:]), "body")
    near = lax.dynamic_slice_in_dim(totals, body_index * local_count, local_count, 0)
    partial_value = complex_apply("iln,inq->lq", scattered, up_maps[:, 0], up_maps[:, 1])
    expansion = lax.psum(partial_value, "body").astype(jnp.bfloat16)
    block_width = group_maps.shape[3]
    full_width = group_maps.shape[4]
    real_block = lax.dynamic_slice_in_dim(expansion, body_index * block_width, block_width, 1)
    imag_block = lax.dynamic_slice_in_dim(
        expansion, full_width + body_index * block_width, block_width, 1
    )
    own_block = jnp.concatenate([real_block, imag_block], axis=-1)[None]
    piece = lax.all_gather(own_block, "grp", axis=0, tiled=True)
    width = piece.shape[0]
    sources = jnp.arange(width, dtype=jnp.int32)
    piece = jnp.where((sources != group_index)[:, None, None], piece, zero_seq)
    mats = group_maps[0]
    incoming_part = complex_apply("hln,hnq->lq", piece, mats[:, 0], mats[:, 1])
    incoming = lax.psum(incoming_part, "body").astype(jnp.bfloat16)
    far = complex_apply("lq,iqp->ilp", incoming, down_maps[:, 0], down_maps[:, 1])
    return exciting + near + far


def solution(mesh):
    return jax.shard_map(
        local,
        mesh=mesh,
        in_specs=(
            P(("grp", "body"), None, None),
            P(("grp", "body"), None, None),
            P(("grp", "body"), None, None, None),
            P(),
            P(("grp", "body"), None),
            P("grp"),
            P(("grp", "body"), None, None, None),
            P(("grp", "body"), None, None, None),
            P("grp", None, None, "body", None),
        ),
        out_specs=P(("grp", "body"), None, None),
        check_vma=False,
    )
```

profile of v0, /device:TPU:32, one launch (start us, length us, event | category | flops | bytes accessed | tf_op | source)
XLA Modules:
  0.0 437.4 jit_solution(12570242964982283185)
XLA Ops:
  8.7 1.3 dynamic_slice.16
  12.1 32.7 %all-gather.1 = s32[32,1,32]{2,1,0:T(1,128)S(1)} all-gather(s32[1,1,32]{2,1,0:T(1,128)} %bitcast.159), channel_id=1, replica_groups=mesh['grp'=16,'body'=32] {'body'}, dimensions={0}, use_global_device_ids=true | all-gather | bytes 4224 | tf_op jit(solution)/shard_map/all_gather | solution.py:48
  44.8 1.3 fusion.67
  49.3 119.1 %while.11 = (s32[]{:T(128)}, f32[8,4,16,512]{3,2,1,0:T(8,128)}, bf16[8,4,1,2,512]{4,3,1,2,0:T(2,128)(2,1)S(1)}, bf16[1,16,512]{2,1,0:T(8,128)(2,1)S(1)}, s32[]{:T(128)}) while((s32[]{:T(128)}, f32[8,4,16,512]{3,2,1,0:T(8,128)}, bf16[8,4,1,2,512]{4,3,1,2,0:T(2,128)(2,1)S(1)}, bf16[1,16,512]{2,1,0:T(8,128)(2,1)S(1)}, s32[]{:T(128)}) %tuple.28), condition=%wide.region_1.2_spmd, body=%wide.region_0.1_spmd.sunk | while | flops 33619968 | bytes 17474112 | solution.py:63
  49.5 2.8 tile.14
  52.3 4.4 %slice.219 = bf16[4,1,2,130816]{3,2,0,1:T(2,128)(2,1)} slice(bf16[4,1,2,131072]{3,2,0,1:T(2,128)(2,1)} %tile.14), slice={[0:4], [0:1], [0:2], [256:131072]} | slice | bytes 4186112 | tf_op jit(solution)/shard_map/while/body/eval_jaxpr/slice | solution.py:25
  56.7 6.1 %reshape.288 = bf16[4,1,2,256,511]{4,3,2,0,1:T(8,128)(2,1)S(1)} reshape(bf16[4,1,2,130816]{3,2,0,1:T(2,128)(2,1)} %slice.219) | data formatting | bytes 4186112 | tf_op jit(solution)/shard_map/while/body/eval_jaxpr/reshape | solution.py:26
  64.4 2.8 tile.14
  67.2 4.4 %slice.219 = bf16[4,1,2,130816]{3,2,0,1:T(2,128)(2,1)} slice(bf16[4,1,2,131072]{3,2,0,1:T(2,128)(2,1)} %tile.14), slice={[0:4], [0:1], [0:2], [256:131072]} | slice | bytes 4186112 | tf_op jit(solution)/shard_map/while/body/eval_jaxpr/slice | solution.py:25
  71.6 6.1 %reshape.288 = bf16[4,1,2,256,511]{4,3,2,0,1:T(8,128)(2,1)S(1)} reshape(bf16[4,1,2,130816]{3,2,0,1:T(2,128)(2,1)} %slice.219) | data formatting | bytes 4186112 | tf_op jit(solution)/shard_map/while/body/eval_jaxpr/reshape | solution.py:26
  79.2 2.8 tile.14
  82.0 4.4 %slice.219 = bf16[4,1,2,130816]{3,2,0,1:T(2,128)(2,1)} slice(bf16[4,1,2,131072]{3,2,0,1:T(2,128)(2,1)} %tile.14), slice={[0:4], [0:1], [0:2], [256:131072]} | slice | bytes 4186112 | tf_op jit(solution)/shard_map/while/body/eval_jaxpr/slice | solution.py:25
  86.4 6.1 %reshape.288 = bf16[4,1,2,256,511]{4,3,2,0,1:T(8,128)(2,1)S(1)} reshape(bf16[4,1,2,130816]{3,2,0,1:T(2,128)(2,1)} %slice.219) | data formatting | bytes 4186112 | tf_op jit(solution)/shard_map/while/body/eval_jaxpr/reshape | solution.py:26
  94.1 2.8 tile.14
  96.9 4.4 %slice.219 = bf16[4,1,2,130816]{3,2,0,1:T(2,128)(2,1)} slice(bf16[4,1,2,131072]{3,2,0,1:T(2,128)(2,1)} %tile.14), slice={[0:4], [0:1], [0:2], [256:131072]} | slice | bytes 4186112 | tf_op jit(solution)/shard_map/while/body/eval_jaxpr/slice | solution.py:25
  101.3 6.1 %reshape.288 = bf16[4,1,2,256,511]{4,3,2,0,1:T(8,128)(2,1)S(1)} reshape(bf16[4,1,2,130816]{3,2,0,1:T(2,128)(2,1)} %slice.219) | data formatting | bytes 4186112 | tf_op jit(solution)/shard_map/while/body/eval_jaxpr/reshape | solution.py:26
  109.0 2.8 tile.14
  111.8 4.4 %slice.219 = bf16[4,1,2,130816]{3,2,0,1:T(2,128)(2,1)} slice(bf16[4,1,2,131072]{3,2,0,1:T(2,128)(2,1)} %tile.14), slice={[0:4], [0:1], [0:2], [256:131072]} | slice | bytes 4186112 | tf_op jit(solution)/shard_map/while/body/eval_jaxpr/slice | solution.py:25
  116.2 6.1 %reshape.288 = bf16[4,1,2,256,511]{4,3,2,0,1:T(8,128)(2,1)S(1)} reshape(bf16[4,1,2,130816]{3,2,0,1:T(2,128)(2,1)} %slice.219) | data formatting | bytes 4186112 | tf_op jit(solution)/shard_map/while/body/eval_jaxpr/reshape | solution.py:26
  123.9 2.8 tile.14
  126.7 4.4 %slice.219 = bf16[4,1,2,130816]{3,2,0,1:T(2,128)(2,1)} slice(bf16[4,1,2,131072]{3,2,0,1:T(2,128)(2,1)} %tile.14), slice={[0:4], [0:1], [0:2], [256:131072]} | slice | bytes 4186112 | tf_op jit(solution)/shard_map/while/body/eval_jaxpr/slice | solution.py:25
  131.1 6.1 %reshape.288 = bf16[4,1,2,256,511]{4,3,2,0,1:T(8,128)(2,1)S(1)} reshape(bf16[4,1,2,130816]{3,2,0,1:T(2,128)(2,1)} %slice.219) | data formatting | bytes 4186112 | tf_op jit(solution)/shard_map/while/body/eval_jaxpr/reshape | solution.py:26
  138.8 2.8 tile.14
  141.6 4.4 %slice.219 = bf16[4,1,2,130816]{3,2,0,1:T(2,128)(2,1)} slice(bf16[4,1,2,131072]{3,2,0,1:T(2,128)(2,1)} %tile.14), slice={[0:4], [0:1], [0:2], [256:131072]} | slice | bytes 4186112 | tf_op jit(solution)/shard_map/while/body/eval_jaxpr/slice | solution.py:25
  146.0 6.1 %reshape.288 = bf16[4,1,2,256,511]{4,3,2,0,1:T(8,128)(2,1)S(1)} reshape(bf16[4,1,2,130816]{3,2,0,1:T(2,128)(2,1)} %slice.219) | data formatting | bytes 4186112 | tf_op jit(solution)/shard_map/while/body/eval_jaxpr/reshape | solution.py:26
  153.6 2.8 tile.14
  156.4 4.4 %slice.219 = bf16[4,1,2,130816]{3,2,0,1:T(2,128)(2,1)} slice(bf16[4,1,2,131072]{3,2,0,1:T(2,128)(2,1)} %tile.14), slice={[0:4], [0:1], [0:2], [256:131072]} | slice | bytes 4186112 | tf_op jit(solution)/shard_map/while/body/eval_jaxpr/slice | solution.py:25
  160.8 6.1 %reshape.288 = bf16[4,1,2,256,511]{4,3,2,0,1:T(8,128)(2,1)S(1)} reshape(bf16[4,1,2,130816]{3,2,0,1:T(2,128)(2,1)} %slice.219) | data formatting | bytes 4186112 | tf_op jit(solution)/shard_map/while/body/eval_jaxpr/reshape | solution.py:26
  169.0 104.8 %psum.22 = bf16[16,1024]{1,0:T(8,128)(2,1)S(1)} all-reduce(f32[16,1024]{1,0:T(8,128)S(1)} %pad_maximum_fusion), channel_id=1, replica_groups=mesh['grp'=16,'body'=32] {'body'}, use_global_device_ids=true, to_apply=%region_3.4 | all-reduce | flops 16384 | bytes 98304 | tf_op jit(solution)/shard_map/psum | solution.py:67
  274.0 48.7 %all-gather = bf16[256,32]{1,0:T(8,128)(2,1)S(1)} all-gather(bf16[16,32]{1,0:T(8,128)(2,1)S(1)} %pad_maximum_fusion.3), channel_id=2, replica_groups=mesh['grp'=16,'body'=32] {'grp'}, dimensions={0}, use_global_device_ids=true | all-gather | bytes 17408 | tf_op jit(solution)/shard_map/all_gather | solution.py:75
  324.0 104.5 %psum.23 = bf16[16,1024]{1,0:T(8,128)(2,1)S(1)} all-reduce(f32[16,1024]{1,0:T(8,128)S(1)} %pad_maximum_fusion.1), channel_id=1, replica_groups=mesh['grp'=16,'body'=32] {'body'}, use_global_device_ids=true, to_apply=%region_4.5 | all-reduce | flops 16384 | bytes 98304 | tf_op jit(solution)/shard_map/psum | solution.py:81
  429.2 1.4 maximum_add_fusion
  (99 shorter events, 20.5 us)
Async XLA Ops:
  6.5 41.9 %copy-start = (bf16[225,2,512]{2,1,0:T(2,128)(2,1)S(1)}, bf16[225,2,512]{2,1,0:T(2,128)(2,1)}, u32[]{:S(2)}) copy-start(bf16[225,2,512]{2,1,0:T(2,128)(2,1)} %param.14) | copy-start | bytes 1382404
  6.5 422.6 %all-reduce.2.cloned.1.call-start = ((), (), s32[]{:S(2)}) async-start(), calls=%async_computation | async-start | bytes 2097152 | tf_op jit(solution)/shard_map/psum | solution.py:64
  49.3 119.1 %copy-start.2 = (bf16[1,2,256,512]{3,2,1,0:T(8,128)(2,1)S(1)}, bf16[1,2,256,512]{3,2,1,0:T(8,128)(2,1)}, u32[]{:S(2)}) copy-start(bf16[1,2,256,512]{3,2,1,0:T(8,128)(2,1)} %param.17) | copy-start | bytes 1572868
  168.4 154.4 %copy-start.3 = (bf16[1,16,2,16,512]{4,3,2,1,0:T(8,128)(2,1)S(1)}, bf16[1,16,2,16,512]{4,3,2,1,0:T(8,128)(2,1)}, u32[]{:S(2)}) copy-start(bf16[1,16,2,16,512]{4,3,2,1,0:T(8,128)(2,1)} %param.19) | copy-start | bytes 1572868
  168.7 259.9 %copy-start.1 = (bf16[1,2,512,256]{3,2,1,0:T(8,128)(2,1)S(1)}, bf16[1,2,512,256]{3,2,1,0:T(8,128)(2,1)}, u32[]{:S(2)}) copy-start(bf16[1,2,512,256]{3,2,1,0:T(8,128)(2,1)} %param.18) | copy-start | bytes 1572868
  322.7 106.4 %copy-start.4 = (f32[1,16,512]{2,1,0:T(8,128)S(1)}, f32[1,16,512]{2,1,0:T(8,128)}, u32[]{:S(2)}) copy-start(f32[1,16,512]{2,1,0:T(8,128)} %param.12) | copy-start | bytes 98308
Sparse Core Ops, SparseCore 0:
  168.5 234.8 all-reduce.1
where the time goes:
time: 438 us; the launch traced here: 437 us
  blocking collectives  291 us (66%)
  local copies, waits for them, and re-layouts  110 us (25%)
  between operations  15.6 us (4%)
  matrix products  12.5 us (3%)
  other arithmetic  8.4 us (2%)
    psum x1, blocking collectives, local(): expansion = lax.psum(partial_value, 'body').astype(jnp.bfloat16)  105 us
    psum x1, blocking collectives, local(): incoming = lax.psum(incoming_part, 'body').astype(jnp.bfloat16)  105 us
    all_gather x1, blocking collectives, local(): piece = lax.all_gather(own_block, 'grp', axis=0, tiled=True)  48.7 us
    reshape x8, local copies, waits for them, and re-layouts, toeplitz_mats(): window.reshape(sequences.shape[:-1] + (length, 2 * length - 1))  48.7 us
    slice x8, local copies, waits for them, and re-layouts, toeplitz_mats(): window = tiled[..., length:length + length * (2 * length - 1)]  35.2 us
    all_gather x1, blocking collectives, local(): all_offsets = lax.all_gather(offsets, 'body', axis=0, tiled=True)  32.7 us
    another operation x24, local copies, waits for them, and re-layouts, toeplitz_mats(): tiled = jnp.tile(sequences, repeats)  23.8 us
  transfers between devices with their start and end apart: 1, of which 0 were waited for; matrix products, arithmetic and copies ran while one was open for 1% of the time, Pallas kernels for 0%

commit v1 on v0

--- a/solution.py
+++ b/solution.py
@@ -78,7 +78,7 @@
     piece = jnp.where((sources != group_index)[:, None, None], piece, zero_seq)
     mats = group_maps[0]
     incoming_part = complex_apply("hln,hnq->lq", piece, mats[:, 0], mats[:, 1])
-    incoming = lax.psum(incoming_part, "body").astype(jnp.bfloat16)
+    incoming = jnp.sum(lax.all_gather(incoming_part, "body"), axis=0).astype(jnp.bfloat16)
     far = complex_apply("lq,iqp->ilp", incoming, down_maps[:, 0], down_maps[:, 1])
     return exciting + near + far
 

time: 438 us -> 564 us (1.29)
  the two profiles are of different devices: /device:TPU:32 before, /device:TPU:1 now
where the time goes in v1:
time: 564 us; the launch traced here: 563 us
  waiting for transfers between devices  222 us (39%)
  blocking collectives  189 us (34%)
  local copies, waits for them, and re-layouts  109 us (19%)
  matrix products  16.4 us (3%)
  between operations  15.5 us (3%)
  other arithmetic  10.8 us (2%)
    psum x1, waiting for transfers between devices, local(): totals = lax.psum(terms.reshape((group_count,) + terms.shape[2:]), 'body')  222 us
    psum x1, blocking collectives, local(): expansion = lax.psum(partial_value, 'body').astype(jnp.bfloat16)  107 us
    reshape x8, local copies, waits for them, and re-layouts, toeplitz_mats(): window.reshape(sequences.shape[:-1] + (length, 2 * length - 1))  48.7 us
    all_gather x1, blocking collectives, local(): all_offsets = lax.all_gather(offsets, 'body', axis=0, tiled=True)  41.5 us
    all_gather x1, blocking collectives, local(): piece = lax.all_gather(own_block, 'grp', axis=0, tiled=True)  40.8 us
    slice x8, local copies, waits for them, and re-layouts, toeplitz_mats(): window = tiled[..., length:length + length * (2 * length - 1)]  35.1 us
    another operation x24, local copies, waits for them, and re-layouts, toeplitz_mats(): tiled = jnp.tile(sequences, repeats)  23.6 us
  transfers between devices with their start and end apart: 2, of which 1 were waited for; matrix products, arithmetic and copies ran while one was open for 22% of the time, Pallas kernels for 0%

profile of v1, /device:TPU:1, one launch (start us, length us, event | category | flops | bytes accessed | tf_op | source)
XLA Modules:
  0.0 562.7 jit_solution(7495215862793995918)
XLA Ops:
  15.4 106.9 %psum.15 = bf16[16,1024]{1,0:T(8,128)(2,1)S(1)} all-reduce(f32[16,1024]{1,0:T(8,128)S(1)} %pad_maximum_fusion), channel_id=1, replica_groups=mesh['grp'=16,'body'=32] {'body'}, use_global_device_ids=true, to_apply=%region_3.4 | all-reduce | flops 16384 | bytes 98304 | tf_op jit(solution)/shard_map/psum | solution.py:67
  122.4 40.8 %all-gather = bf16[256,32]{1,0:T(8,128)(2,1)S(1)} all-gather(bf16[16,32]{1,0:T(8,128)(2,1)S(1)} %pad_maximum_fusion.3), channel_id=2, replica_groups=mesh['grp'=16,'body'=32] {'grp'}, dimensions={0}, use_global_device_ids=true | all-gather | bytes 17408 | tf_op jit(solution)/shard_map/all_gather | solution.py:75
  167.9 41.5 %all-gather.2 = s32[32,1,32]{2,1,0:T(1,128)S(1)} all-gather(s32[1,1,32]{2,1,0:T(1,128)S(1)} %bitcast.161), channel_id=1, replica_groups=mesh['grp'=16,'body'=32] {'body'}, dimensions={0}, use_global_device_ids=true | all-gather | bytes 4224 | tf_op jit(solution)/shard_map/all_gather | solution.py:48
  209.4 1.3 fusion.67
  211.7 118.9 %while.11 = (s32[]{:T(128)}, f32[8,4,16,512]{3,2,1,0:T(8,128)}, bf16[8,4,1,2,512]{4,3,1,2,0:T(2,128)(2,1)S(1)}, bf16[1,16,512]{2,1,0:T(8,128)(2,1)S(1)}, s32[]{:T(128)}) while((s32[]{:T(128)}, f32[8,4,16,512]{3,2,1,0:T(8,128)}, bf16[8,4,1,2,512]{4,3,1,2,0:T(2,128)(2,1)S(1)}, bf16[1,16,512]{2,1,0:T(8,128)(2,1)S(1)}, s32[]{:T(128)}) %tuple.28), condition=%wide.region_1.2_spmd, body=%wide.region_0.1_spmd.sunk | while | flops 33619968 | bytes 17474112 | solution.py:63
  211.9 2.8 tile.14
  214.7 4.4 slice.219
  219.1 6.1 %reshape.289 = bf16[4,1,2,256,511]{4,3,2,0,1:T(8,128)(2,1)S(1)} reshape(bf16[4,1,2,130816]{3,2,0,1:T(2,128)(2,1)} %slice.219) | data formatting | bytes 4186112 | tf_op jit(solution)/shard_map/while/body/eval_jaxpr/reshape | solution.py:26
  226.8 2.8 tile.14
  229.5 4.4 slice.219
  233.9 6.1 %reshape.289 = bf16[4,1,2,256,511]{4,3,2,0,1:T(8,128)(2,1)S(1)} reshape(bf16[4,1,2,130816]{3,2,0,1:T(2,128)(2,1)} %slice.219) | data formatting | bytes 4186112 | tf_op jit(solution)/shard_map/while/body/eval_jaxpr/reshape | solution.py:26
  241.6 2.8 tile.14
  244.4 4.4 slice.219
  248.8 6.1 %reshape.289 = bf16[4,1,2,256,511]{4,3,2,0,1:T(8,128)(2,1)S(1)} reshape(bf16[4,1,2,130816]{3,2,0,1:T(2,128)(2,1)} %slice.219) | data formatting | bytes 4186112 | tf_op jit(solution)/shard_map/while/body/eval_jaxpr/reshape | solution.py:26
  256.5 2.8 tile.14
  259.3 4.4 slice.219
  263.6 6.1 %reshape.289 = bf16[4,1,2,256,511]{4,3,2,0,1:T(8,128)(2,1)S(1)} reshape(bf16[4,1,2,130816]{3,2,0,1:T(2,128)(2,1)} %slice.219) | data formatting | bytes 4186112 | tf_op jit(solution)/shard_map/while/body/eval_jaxpr/reshape | solution.py:26
  271.3 2.8 tile.14
  274.1 4.4 slice.219
  278.5 6.1 %reshape.289 = bf16[4,1,2,256,511]{4,3,2,0,1:T(8,128)(2,1)S(1)} reshape(bf16[4,1,2,130816]{3,2,0,1:T(2,128)(2,1)} %slice.219) | data formatting | bytes 4186112 | tf_op jit(solution)/shard_map/while/body/eval_jaxpr/reshape | solution.py:26
  286.2 2.8 tile.14
  289.0 4.4 slice.219
  293.4 6.1 %reshape.289 = bf16[4,1,2,256,511]{4,3,2,0,1:T(8,128)(2,1)S(1)} reshape(bf16[4,1,2,130816]{3,2,0,1:T(2,128)(2,1)} %slice.219) | data formatting | bytes 4186112 | tf_op jit(solution)/shard_map/while/body/eval_jaxpr/reshape | solution.py:26
  301.0 2.8 tile.14
  303.8 4.4 slice.219
  308.2 6.1 %reshape.289 = bf16[4,1,2,256,511]{4,3,2,0,1:T(8,128)(2,1)S(1)} reshape(bf16[4,1,2,130816]{3,2,0,1:T(2,128)(2,1)} %slice.219) | data formatting | bytes 4186112 | tf_op jit(solution)/shard_map/while/body/eval_jaxpr/reshape | solution.py:26
  315.9 2.8 tile.14
  318.7 4.4 slice.219
  323.1 6.1 %reshape.289 = bf16[4,1,2,256,511]{4,3,2,0,1:T(8,128)(2,1)S(1)} reshape(bf16[4,1,2,130816]{3,2,0,1:T(2,128)(2,1)} %slice.219) | data formatting | bytes 4186112 | tf_op jit(solution)/shard_map/while/body/eval_jaxpr/reshape | solution.py:26
  330.6 1.8 reduce_sum.9
  333.0 221.5 %all-reduce.2.cloned.1.call-done = f32[32,16,512]{2,1,0:T(8,128)} async-done(((f32[32,16,512]{2,1,0:T(8,128)}), f32[32,16,512]{2,1,0:T(8,128)}) %all-reduce.2.cloned.1.call-update) | async-done | bytes 1048592 | tf_op jit(solution)/shard_map/psum | solution.py:64
  554.5 1.4 maximum_add_fusion
  (104 shorter events, 25.8 us)
Async XLA Ops:
  6.5 204.3 %copy-start = (bf16[225,2,512]{2,1,0:T(2,128)(2,1)S(1)}, bf16[225,2,512]{2,1,0:T(2,128)(2,1)}, u32[]{:S(2)}) copy-start(bf16[225,2,512]{2,1,0:T(2,128)(2,1)} %param.14) | copy-start | bytes 1382404
  6.5 156.6 %copy-start.2 = (bf16[1,16,2,16,512]{4,3,2,1,0:T(8,128)(2,1)S(1)}, bf16[1,16,2,16,512]{4,3,2,1,0:T(8,128)(2,1)}, u32[]{:S(2)}) copy-start(bf16[1,16,2,16,512]{4,3,2,1,0:T(8,128)(2,1)} %param.19) | copy-start | bytes 1572868
  6.5 324.1 %all-gather.5.cloned.1.call-start = ((), (), s32[]{:S(2)}) async-start(), calls=%async_computation.1 | async-start | bytes 2162688 | tf_op jit(solution)/shard_map/all_gather | solution.py:81
  13.1 152.1 %copy-start.5 = (s32[32]{0:T(128)S(1)}, s32[32]{0:T(128)}, u32[]{:S(2)}) copy-start(s32[32]{0:T(128)} %param.16) | copy-start | bytes 388
  13.1 154.8 %copy-start.4 = (s32[1,32]{1,0:T(1,128)S(1)}, s32[1,32]{1,0:T(1,128)}, u32[]{:S(2)}) copy-start(s32[1,32]{1,0:T(1,128)} %param.15) | copy-start | bytes 388
  165.1 389.4 %all-reduce.2.cloned.1.call-start = ((), (), s32[]{:S(2)}) async-start(), calls=%async_computation | async-start | bytes 2097152 | tf_op jit(solution)/shard_map/psum | solution.py:64
  330.6 1.8 copy-start.1
  330.6 223.9 %copy-start.3 = (f32[1,16,512]{2,1,0:T(8,128)S(1)}, f32[1,16,512]{2,1,0:T(8,128)}, u32[]{:S(2)}) copy-start(f32[1,16,512]{2,1,0:T(8,128)} %param.12) | copy-start | bytes 98308
Sparse Core Ops, SparseCore 0:
  165.2 69.3 all-gather.4
  330.7 223.7 all-reduce.1
